TPU v7x, 512 devices: a whole 4x8x8 slice. The times are simulated.
512 devices in a mesh: wide: 32 (over z, x), narrow: 16 (over y, core).
Axes of the slice: x: 4, y: 8, z: 8, core: 2. Of those that a mesh axis runs over, the one named last changes fastest.
Arguments:
- embeddings: bfloat16 [262144, 1024], P(('wide', 'narrow')), may hold values from -32 to 32
- valid: int32 [262144], P(('wide', 'narrow')), may hold values from 0 to 1, as said below
Outputs:
- whitened: bfloat16 [262144, 1024], P(('wide', 'narrow'))
Inputs may be any that keep to these rules, and one draw needn't show every extreme that they name: The first row of every aligned block of 16 rows has valid = 1.
All inputs are finite; a program needn't handle non-finite values.
Results may differ from a plain program's by a relative error of at most 0.001.
Values sent between devices are 32-bit elements; how exact they have to be, the bound alone decides.
A program may use at most 64 MiB of HBM per device.

v0:
```python
import jax
import jax.numpy as jnp
from jax import lax
from jax.sharding import PartitionSpec as P


def merged(part, axis, combine):
    gathered = jax.tree.map(lambda a: lax.all_gather(a, axis), part)

    def take(source):
        return jax.tree.map(lambda a: lax.dynamic_index_in_dim(a, source, 0, False), gathered)

    return lax.fori_loop(
        1, lax.axis_size(axis), lambda source, state: combine(state, take(source)), take(0)
    )


def shifted_scatter(gram, count_local, sums_local, center):
    return (
        gram
        - sums_local[:, None] * center[None, :]
        - center[:, None] * sums_local[None, :]
        + count_local * center[:, None] * center[None, :]
    )


def narrow_rows(term):
    return lax.psum_scatter(term, "narrow", scatter_dimension=0, tiled=True)


def on_device(embeddings, valid):
    width = embeddings.shape[1]
    narrow_count = lax.axis_size("narrow")
    row_span = width // narrow_count
    offset = lax.axis_index("narrow") * row_span
    mask_half = valid.astype(jnp.bfloat16)
    count_local = jnp.sum(valid.astype(jnp.float32))
    masked = embeddings * mask_half[:, None]
    gram = lax.dot_general(
        masked, embeddings, (((0,), (0,)), ((), ())), preferred_element_type=jnp.float32
    )
    sums_local = jnp.dot(mask_half[None, :], embeddings, preferred_element_type=jnp.float32)[0]
    group_count, group_sums = lax.psum((count_local, sums_local), "narrow")
    group_center = group_sums / group_count
    term = shifted_scatter(gram, count_local, sums_local, group_center)
    group_rows = narrow_rows(term)

    def pooled(left, right):
        left_count, left_sums, left_rows = left
        right_count, right_sums, right_rows = right
        joined = left_count + right_count
        shifts = left_sums / left_count - right_sums / right_count
        shift_rows = lax.dynamic_slice_in_dim(shifts, offset, row_span, 0)
        extra = left_count * right_count / joined * shift_rows[:, None] * shifts[None, :]
        return (joined, left_sums + right_sums, left_rows + right_rows + extra)

    count, sums, own_rows = merged((group_count, group_sums, group_rows), "wide", pooled)
    center = sums / count
    cov_rows = own_rows / count
    ident_rows = (
        lax.broadcasted_iota(jnp.int32, (row_span, width), 0) + offset
        == lax.broadcasted_iota(jnp.int32, (row_span, width), 1)
    ).astype(jnp.float32)
    diag_block = lax.dynamic_slice_in_dim(cov_rows, offset, row_span, 1)
    trace_part = jnp.sum(jnp.diagonal(diag_block))
    square_part = jnp.sum(cov_rows * cov_rows)
    trace_cov, square_sum = lax.psum((trace_part, square_part), "narrow")
    ridge_add = 0.05 * trace_cov / width + 1e-06
    norm_frob = jnp.sqrt(square_sum + 2.0 * ridge_add * trace_cov + width * ridge_add * ridge_add)
    base_rows = (cov_rows + ridge_add * ident_rows) / norm_frob
    root_rows = (3.0 * ident_rows - base_rows) / 2.0
    root_full = lax.all_gather(root_rows, "narrow", axis=0, tiled=True)
    first = jnp.dot(
        base_rows, root_full, precision=lax.Precision.HIGHEST, preferred_element_type=jnp.float32
    )
    second = jnp.dot(
        first, root_full, precision=lax.Precision.HIGHEST, preferred_element_type=jnp.float32
    )
    factor = (3.0 * ident_rows - second) / 2.0
    root_rows = jnp.dot(
        factor, root_full, precision=lax.Precision.HIGHEST, preferred_element_type=jnp.float32
    )
    centered_x = embeddings.astype(jnp.float32) - center
    product = jnp.dot(
        centered_x,
        lax.all_gather(root_rows, "narrow", axis=0, tiled=True),
        precision=lax.Precision.HIGHEST,
        preferred_element_type=jnp.float32,
    )
    return (product / jnp.sqrt(norm_frob)).astype(jnp.bfloat16)


def solution(mesh):
    in_specs = (P(("wide", "narrow"), None), P(("wide", "narrow")))
    out_specs = P(("wide", "narrow"), None)
    return jax.shard_map(
        on_device, mesh=mesh, in_specs=in_specs, out_specs=out_specs, check_vma=False
    )
```

profile of v0, /device:TPU:1, one launch (start us, length us, event | category | flops | bytes accessed | tf_op | source)
XLA Modules:
  0.0 490.2 jit_solution(10090267257957100686)
XLA Ops:
  6.5 0.7 convert_element_type.15
  7.2 1.3 convert_reduce_fusion
  8.5 1.5 fusion.12
  10.0 30.9 %all-reduce.2 = (f32[]{:T(128)}, f32[1024]{0:T(1024)S(1)}) all-reduce(f32[]{:T(128)} %convert_reduce_fusion, f32[1024]{0:T(1024)S(1)} %bitcast.31), channel_id=1, replica_groups=mesh['wide'=32,'narrow'=16] {'narrow'}, use_global_device_ids=true, to_apply=%region_1.0 | all-reduce | flops 1025 | bytes 8200 | tf_op jit(solution)/shard_map/psum | solution.py:43
  40.8 1.3 broadcast_multiply_fusion
  42.1 5.4 %multiply_add_fusion = f32[1024,1024]{1,0:T(8,128)} fusion(bf16[512,1024]{1,0:T(8,128)(2,1)} %param.4, f32[1024]{0:T(1024)S(1)} %get-tuple-element.284, f32[1024]{0:T(1024)S(1)} %bitcast.32, f32[1024]{0:T(1024)S(1)} %get-tuple-element.285, bf16[512]{0:T(512)(128)(2,1)S(1)} %convert_element_type.15), kind=kOutput, calls=%fused_computation.6 | convolution fusion | flops 1080557568 | bytes 5256192 | tf_op jit(solution)/shard_map/dot_general | solution.py:39
  47.6 62.6 %reduce-scatter.2.cloned.1.call-done = f32[64,1024]{1,0:T(8,128)} async-done(((f32[1024,1024]{1,0:T(8,128)}), f32[64,1024]{1,0:T(8,128)}) %reduce-scatter.2.cloned.1.call-update) | async-done | bytes 262160 | tf_op jit(solution)/shard_map/reduce_scatter | solution.py:28
  110.2 35.0 %all-gather = f32[32768]{0:T(1024)S(1)} all-gather(f32[1024]{0:T(1024)S(1)} %get-tuple-element.281), channel_id=2, replica_groups=mesh['wide'=32,'narrow'=16] {'wide'}, dimensions={0}, use_global_device_ids=true | all-gather | bytes 135168 | tf_op jit(solution)/shard_map/all_gather | solution.py:8
  145.3 1.3 dynamic-slice
  146.6 1.3 dynamic-update-slice
  147.9 59.3 %all-reduce = f32[32]{0:T(128)S(1)} all-reduce(f32[32]{0:T(128)S(1)} %dynamic-update-slice), channel_id=1, replica_groups=mesh['wide'=32,'narrow'=16] {'wide'}, use_global_device_ids=true, to_apply=%add | all-reduce | flops 32 | bytes 256
  207.2 11.9 %all-gather.10.cloned.1.call-done = f32[2048,1024]{1,0:T(8,128)} async-done(((f32[64,1024]{1,0:T(8,128)}), f32[2048,1024]{1,0:T(8,128)}) %all-gather.10.cloned.1.call-update) | async-done | bytes 8388624 | tf_op jit(solution)/shard_map/all_gather | solution.py:8
  219.1 1.0 slice.8
  220.1 116.4 %while.21 = (s32[]{:T(128)}, f32[]{:T(128)}, f32[1024]{0:T(1024)S(1)}, f32[64,1024]{1,0:T(8,128)S(1)}, f32[32]{0:T(128)S(1)}, /*index=5*/f32[32,1024]{1,0:T(8,12...) while((s32[]{:T(128)}, f32[]{:T(128)}, f32[1024]{0:T(1024)S(1)}, ...), condition=%wide.region_5.6_spmd, body=%wide.region_4.5_spmd.sunk | while | flops 200776 | bytes 816103 | solution.py:13
  222.1 0.7 divide_subtract_fusion.2
  222.8 1.0 fusion.24
  226.6 1.0 fusion.24
  230.3 1.0 fusion.24
  233.3 0.7 divide_subtract_fusion.2
  234.1 1.0 fusion.24
  237.1 0.7 divide_subtract_fusion.2
  237.8 1.0 fusion.24
  241.6 1.0 fusion.24
  245.3 1.0 fusion.24
  249.1 1.0 fusion.24
  252.1 0.7 divide_subtract_fusion.2
  252.8 1.0 fusion.24
  255.8 0.7 divide_subtract_fusion.2
  256.6 1.0 fusion.24
  260.3 1.0 fusion.24
  264.1 1.0 fusion.24
  267.1 0.7 divide_subtract_fusion.2
  267.8 1.0 fusion.24
  270.9 0.7 divide_subtract_fusion.2
  271.6 1.0 fusion.24
  274.6 0.7 divide_subtract_fusion.2
  275.4 1.0 fusion.24
  279.1 1.0 fusion.24
  282.9 1.0 fusion.24
  286.6 1.0 fusion.24
  290.4 1.0 fusion.24
  294.1 1.0 fusion.24
  297.9 1.0 fusion.24
  301.6 1.0 fusion.24
  305.4 1.0 fusion.24
  309.1 1.0 fusion.24
  312.9 1.0 fusion.24
  316.6 1.0 fusion.24
  320.4 1.0 fusion.24
  324.1 1.0 fusion.24
  327.9 1.0 fusion.24
  331.7 1.0 fusion.24
  335.4 1.0 fusion.24
  336.5 0.7 multiply_reduce_fusion
  337.2 0.8 gather_fusion
  338.0 0.7 reduce_sum.28
  338.7 37.7 %all-reduce.1 = (f32[]{:T(128)}, f32[]{:T(128)}) all-reduce(f32[]{:T(128)} %get-tuple-element.282, f32[]{:T(128)} %reduce_sum.28), channel_id=1, replica_groups=mesh['wide'=32,'narrow'=16] {'narrow'}, use_global_device_ids=true, to_apply=%region_9.10 | all-reduce | flops 2 | bytes 16 | tf_op jit(solution)/shard_map/psum | solution.py:67
  378.5 0.8 fusion.10
  379.6 39.5 %all-gather.6.cloned.1.call-done = f32[1024,1024]{1,0:T(8,128)} async-done(((f32[64,1024]{1,0:T(8,128)}), f32[1024,1024]{1,0:T(8,128)}) %all-gather.6.cloned.1.call-update) | async-done | bytes 4194320 | tf_op jit(solution)/shard_map/all_gather | solution.py:72
  419.1 5.0 %fusion.11 = f32[64,1024]{1,0:T(8,128)S(1)} fusion(f32[1024,1024]{1,0:T(8,128)} %all-gather.6.cloned.1.call-done, f32[64,1024]{1,0:T(8,128)S(1)} %get-tuple-element.283, f32[]{:T(128)S(6)} %sqrt.6, f32[]{:T(128)S(6)} %add.145, s32[64]{0:T(128)S(1)} %iota_add_fusion), kind=kOutput, calls=%fused_computation.29 | convolution fusion | flops 805568512 | bytes 4718856 | tf_op jit(solution)/shard_map/dot_general | solution.py:73
  424.2 2.7 fusion.7
  426.8 3.4 fusion.13
  430.2 43.9 %all-gather.8.cloned.1.call-done = f32[1024,1024]{1,0:T(8,128)} async-done(((f32[64,1024]{1,0:T(8,128)}), f32[1024,1024]{1,0:T(8,128)}) %all-gather.8.cloned.1.call-update) | async-done | bytes 4194320 | tf_op jit(solution)/shard_map/all_gather | solution.py:86
  474.1 9.6 %divide_convert_fusion = bf16[512,1024]{1,0:T(8,128)(2,1)} fusion(f32[1024,1024]{1,0:T(8,128)} %all-gather.8.cloned.1.call-done, bf16[512,1024]{1,0:T(8,128)(2,1)S(1)} %copy-done.1, f32[]{:T(128)S(6)} %sqrt.7, f32[1024]{0:T(1024)S(1)} %broadcast_divide_fusion.1), kind=kOutput, calls=%fused_computation.7 | convolution fusion | flops 6444548096 | bytes 6295556 | tf_op jit(solution)/shard_map/dot_general | solution.py:84
  (136 shorter events, 36.7 us)
Async XLA Ops:
  6.5 103.6 %reduce-scatter.2.cloned.1.call-start = ((), (), s32[]{:S(2)}) async-start(), calls=%async_computation.1 | async-start | bytes 4456448 | tf_op jit(solution)/shard_map/reduce_scatter | solution.py:28
  47.5 171.6 %all-gather.10.cloned.1.call-start = ((), (), s32[]{:S(2)}) async-start(), calls=%async_computation.4 | async-start | bytes 8650752 | tf_op jit(solution)/shard_map/all_gather | solution.py:8
  110.2 308.9 %all-gather.6.cloned.1.call-start = ((), (), s32[]{:S(2)}) async-start(), calls=%async_computation.2 | async-start | bytes 4456448 | tf_op jit(solution)/shard_map/all_gather | solution.py:72
  379.4 94.7 %all-gather.8.cloned.1.call-start = ((), (), s32[]{:S(2)}) async-start(), calls=%async_computation.3 | async-start | bytes 4456448 | tf_op jit(solution)/shard_map/all_gather | solution.py:86
  419.1 5.0 %copy-start = (f32[1024,1024]{1,0:T(8,128)S(1)}, f32[1024,1024]{1,0:T(8,128)}, u32[]{:S(2)}) copy-start(f32[1024,1024]{1,0:T(8,128)} %all-gather.6.cloned.1.call-done) | copy-start | bytes 12582916
  424.1 50.0 %copy-start.1 = (bf16[512,1024]{1,0:T(8,128)(2,1)S(1)}, bf16[512,1024]{1,0:T(8,128)(2,1)}, u32[]{:S(2)}) copy-start(bf16[512,1024]{1,0:T(8,128)(2,1)} %param.4) | copy-start | bytes 3145732
Sparse Core Ops, SparseCore 0:
  47.6 62.4 reduce-scatter.1
  113.3 105.7 all-gather.9
  379.5 39.5 all-gather.5
  430.3 43.7 all-gather.7
where the time goes:
time: 494 us; the launch traced here: 490 us
  blocking collectives  163 us (33%)
  waiting for transfers between devices  158 us (32%)
  other arithmetic  60.5 us (12%)
  loops' own time  42.7 us (9%)
  matrix products  27.4 us (6%)
  local copies, waits for them, and re-layouts  23.1 us (5%)
  between operations  15.4 us (3%)
    reduce_scatter x1, waiting for transfers between devices, narrow_rows(): return lax.psum_scatter(term, 'narrow', scatter_dimension=0, tiled=True)  62.6 us
    unnamed x1, blocking collectives  59.3 us
    all_gather x1, waiting for transfers between devices, on_device(): lax.all_gather(root_rows, 'narrow', axis=0, tiled=True)  43.9 us
    another operation x1, loops' own time, merged(): lax.fori_loop(1, lax.axis_size(axis), lambda source, state: combine(state...  42.7 us
    all_gather x1, waiting for transfers between devices, on_device(): root_full = lax.all_gather(root_rows, 'narrow', axis=0, tiled=True)  39.5 us
    psum x1, blocking collectives, on_device(): trace_cov, square_sum = lax.psum((trace_part, square_part), 'narrow')  37.7 us
    all_gather x1, blocking collectives, merged(): gathered = jax.tree.map(lambda a: lax.all_gather(a, axis), part)  35 us
    add x31, other arithmetic, pooled(): return (joined, left_sums + right_sums, left_rows + right_rows + extra)  32.3 us
  transfers between devices with their start and end apart: 4, of which 4 were waited for; matrix products, arithmetic and copies ran while one was open for 1% of the time, Pallas kernels for 0%

commit v1 on v0

--- a/solution.py
+++ b/solution.py
@@ -83,7 +83,9 @@
     centered_x = embeddings.astype(jnp.float32) - center
     product = jnp.dot(
         centered_x,
-        lax.all_gather(root_rows, "narrow", axis=0, tiled=True),
+        jnp.concatenate(
+            lax.all_to_all(jnp.stack([root_rows] * lax.axis_size("narrow")), "narrow", 0, 0), axis=0
+        ),
         precision=lax.Precision.HIGHEST,
         preferred_element_type=jnp.float32,
     )

time: 494 us -> 551 us (1.12)
  waiting for transfers between devices: 158 us -> 208 us
    all_to_all x0 -> x1, waiting for transfers between devices: none -> 93.5 us  [on_device(): lax.all_to_all(jnp.stack([root_rows] * lax.axis_size('narrow')), 'narrow'...]
    all_gather x1 -> x0, waiting for transfers between devices: 43.9 us -> none  [on_device(): lax.all_gather(root_rows, 'narrow', axis=0, tiled=True)]
  transfers between devices with their start and end apart: 4 -> 4, of which waited for: 4 -> 4; matrix products, arithmetic and copies ran while one was open for 1% -> 0% of each run, Pallas kernels for 0% -> 0%
where the time goes in v1:
time: 551 us; the launch traced here: 547 us
  waiting for transfers between devices  208 us (38%)
  blocking collectives  163 us (30%)
  other arithmetic  60.6 us (11%)
  loops' own time  42.7 us (8%)
  matrix products  26.7 us (5%)
  local copies, waits for them, and re-layouts  25.6 us (5%)
  between operations  15.4 us (3%)
    all_to_all x1, waiting for transfers between devices, on_device(): lax.all_to_all(jnp.stack([root_rows] * lax.axis_size('narrow')), 'narrow'...  93.5 us
    reduce_scatter x1, waiting for transfers between devices, narrow_rows(): return lax.psum_scatter(term, 'narrow', scatter_dimension=0, tiled=True)  62.5 us
    unnamed x1, blocking collectives  59.2 us
    another operation x1, loops' own time, merged(): lax.fori_loop(1, lax.axis_size(axis), lambda source, state: combine(state...  42.7 us
    all_gather x1, waiting for transfers between devices, on_device(): root_full = lax.all_gather(root_rows, 'narrow', axis=0, tiled=True)  39.9 us
    psum x1, blocking collectives, on_device(): trace_cov, square_sum = lax.psum((trace_part, square_part), 'narrow')  37.6 us
    all_gather x1, blocking collectives, merged(): gathered = jax.tree.map(lambda a: lax.all_gather(a, axis), part)  35.2 us
    add x31, other arithmetic, pooled(): return (joined, left_sums + right_sums, left_rows + right_rows + extra)  32.4 us
  transfers between devices with their start and end apart: 4, of which 4 were waited for; matrix products, arithmetic and copies ran while one was open for 0% of the time, Pallas kernels for 0%

profile of v1, /device:TPU:1, one launch (start us, length us, event | category | flops | bytes accessed | tf_op | source)
XLA Modules:
  0.0 546.9 jit_solution(10098921579468845401)
XLA Ops:
  6.5 0.7 convert_element_type.15
  7.2 1.3 convert_reduce_fusion
  8.5 1.5 fusion.12
  10.0 30.9 %all-reduce.2 = (f32[]{:T(128)}, f32[1024]{0:T(1024)S(1)}) all-reduce(f32[]{:T(128)} %convert_reduce_fusion, f32[1024]{0:T(1024)S(1)} %bitcast.32), channel_id=1, replica_groups=mesh['wide'=32,'narrow'=16] {'narrow'}, use_global_device_ids=true, to_apply=%region_1.0 | all-reduce | flops 1025 | bytes 8200 | tf_op jit(solution)/shard_map/psum | solution.py:43
  40.8 1.3 broadcast_multiply_fusion
  42.1 5.3 multiply_add_fusion
  47.5 62.5 %reduce-scatter.2.cloned.1.call-done = f32[64,1024]{1,0:T(8,128)} async-done(((f32[1024,1024]{1,0:T(8,128)}), f32[64,1024]{1,0:T(8,128)}) %reduce-scatter.2.cloned.1.call-update) | async-done | bytes 262160 | tf_op jit(solution)/shard_map/reduce_scatter | solution.py:28
  110.1 35.2 %all-gather = f32[32768]{0:T(1024)S(1)} all-gather(f32[1024]{0:T(1024)S(1)} %get-tuple-element.281), channel_id=2, replica_groups=mesh['wide'=32,'narrow'=16] {'wide'}, dimensions={0}, use_global_device_ids=true | all-gather | bytes 135168 | tf_op jit(solution)/shard_map/all_gather | solution.py:8
  145.3 1.3 dynamic-slice
  146.6 1.3 dynamic-update-slice
  147.8 59.2 %all-reduce = f32[32]{0:T(128)S(1)} all-reduce(f32[32]{0:T(128)S(1)} %dynamic-update-slice), channel_id=1, replica_groups=mesh['wide'=32,'narrow'=16] {'wide'}, use_global_device_ids=true, to_apply=%add | all-reduce | flops 32 | bytes 256
  207.1 11.9 %all-gather.7.cloned.1.call-done = f32[2048,1024]{1,0:T(8,128)} async-done(((f32[64,1024]{1,0:T(8,128)}), f32[2048,1024]{1,0:T(8,128)}) %all-gather.7.cloned.1.call-update) | async-done | bytes 8388624 | tf_op jit(solution)/shard_map/all_gather | solution.py:8
  219.0 1.0 slice.8
  220.0 116.5 %while.21 = (s32[]{:T(128)}, f32[]{:T(128)}, f32[1024]{0:T(1024)S(1)}, f32[64,1024]{1,0:T(8,128)S(1)}, f32[32]{0:T(128)S(1)}, /*index=5*/f32[32,1024]{1,0:T(8,12...) while((s32[]{:T(128)}, f32[]{:T(128)}, f32[1024]{0:T(1024)S(1)}, ...), condition=%wide.region_5.6_spmd, body=%wide.region_4.5_spmd.sunk | while | flops 200776 | bytes 816103 | solution.py:13
  222.0 0.7 divide_subtract_fusion.2
  222.7 1.0 fusion.24
  225.7 0.7 divide_subtract_fusion.2
  226.5 1.0 fusion.24
  230.2 1.0 fusion.24
  233.3 0.7 divide_subtract_fusion.2
  234.0 1.0 fusion.24
  237.0 0.7 divide_subtract_fusion.2
  237.8 1.0 fusion.24
  241.5 1.0 fusion.24
  244.5 0.7 divide_subtract_fusion.2
  245.3 1.0 fusion.24
  248.3 0.7 divide_subtract_fusion.2
  249.0 1.0 fusion.24
  252.8 1.0 fusion.24
  256.6 1.0 fusion.24
  260.3 1.0 fusion.24
  264.1 1.0 fusion.24
  267.8 1.0 fusion.24
  271.6 1.0 fusion.24
  275.4 1.0 fusion.24
  279.1 1.0 fusion.24
  282.9 1.0 fusion.24
  286.6 1.0 fusion.24
  290.4 1.0 fusion.24
  294.2 1.0 fusion.24
  297.9 1.0 fusion.24
  301.7 1.0 fusion.24
  305.4 1.0 fusion.24
  309.2 1.0 fusion.24
  313.0 1.0 fusion.24
  316.7 1.0 fusion.24
  320.5 1.0 fusion.24
  324.2 1.0 fusion.24
  328.0 1.0 fusion.24
  331.7 1.0 fusion.24
  335.5 1.0 fusion.24
  336.6 0.7 multiply_reduce_fusion
  337.3 0.8 gather_fusion
  338.1 0.7 reduce_sum.28
  338.8 37.6 %all-reduce.1 = (f32[]{:T(128)}, f32[]{:T(128)}) all-reduce(f32[]{:T(128)} %get-tuple-element.282, f32[]{:T(128)} %reduce_sum.28), channel_id=1, replica_groups=mesh['wide'=32,'narrow'=16] {'narrow'}, use_global_device_ids=true, to_apply=%region_9.10 | all-reduce | flops 2 | bytes 16 | tf_op jit(solution)/shard_map/psum | solution.py:67
  378.5 0.8 fusion.10
  379.4 39.9 %all-gather.5.cloned.1.call-done = f32[1024,1024]{1,0:T(8,128)} async-done(((f32[64,1024]{1,0:T(8,128)}), f32[1024,1024]{1,0:T(8,128)}) %all-gather.5.cloned.1.call-update) | async-done | bytes 4194320 | tf_op jit(solution)/shard_map/all_gather | solution.py:72
  419.3 5.0 fusion.11
  424.3 2.6 fusion.7
  427.0 2.6 fusion.13
  429.6 2.5 stack.2
  432.1 5.0 all-to-all-start
  437.2 93.5 %all-to-all-done = f32[16,64,1024]{2,1,0:T(8,128)} async-done(((f32[16,64,1024]{2,1,0:T(8,128)}), f32[16,64,1024]{2,1,0:T(8,128)}, u32[]{:S(2)}, u32[]{:S(2)}) %all-to-all-start) | async-done | bytes 4194336 | tf_op jit(solution)/shard_map/all_to_all | solution.py:87
  530.7 9.6 %divide_convert_fusion = bf16[512,1024]{1,0:T(8,128)(2,1)} fusion(f32[1024,1024]{1,0:T(8,128)} %bitcast.9, bf16[512,1024]{1,0:T(8,128)(2,1)S(1)} %copy-done.1, f32[]{:T(128)S(6)} %sqrt.7, f32[1024]{0:T(1024)S(1)} %broadcast_divide_fusion.1), kind=kOutput, calls=%fused_computation.7 | convolution fusion | flops 6444548096 | bytes 6295556 | tf_op jit(solution)/shard_map/dot_general | solution.py:84
  (136 shorter events, 37.7 us)
Async XLA Ops:
  6.5 103.5 %reduce-scatter.2.cloned.1.call-start = ((), (), s32[]{:S(2)}) async-start(), calls=%async_computation.2 | async-start | bytes 4456448 | tf_op jit(solution)/shard_map/reduce_scatter | solution.py:28
  47.5 171.6 %all-gather.7.cloned.1.call-start = ((), (), s32[]{:S(2)}) async-start(), calls=%async_computation.4 | async-start | bytes 8650752 | tf_op jit(solution)/shard_map/all_gather | solution.py:8
  110.0 309.3 %all-gather.5.cloned.1.call-start = ((), (), s32[]{:S(2)}) async-start(), calls=%async_computation.3 | async-start | bytes 4456448 | tf_op jit(solution)/shard_map/all_gather | solution.py:72
  419.3 5.0 copy-start
  432.1 98.6 %copy-start.1 = (bf16[512,1024]{1,0:T(8,128)(2,1)S(1)}, bf16[512,1024]{1,0:T(8,128)(2,1)}, u32[]{:S(2)}) copy-start(bf16[512,1024]{1,0:T(8,128)(2,1)} %param.4) | copy-start | bytes 3145732
  432.1 98.6 %all-to-all-start = ((f32[16,64,1024]{2,1,0:T(8,128)}), f32[16,64,1024]{2,1,0:T(8,128)}, u32[]{:S(2)}, u32[]{:S(2)}) async-start(f32[16,64,1024]{2,1,0:T(8,128)} %stack.2), calls=%async_computation.1 | async-start | bytes 8388608 | tf_op jit(solution)/shard_map/all_to_all | solution.py:87
Sparse Core Ops, SparseCore 0:
  47.6 62.3 reduce-scatter.1
  113.2 105.8 all-gather.6
  379.5 39.7 all-gather.4
